TPU v7x, 32 devices: a whole 2x2x4 slice. The times are simulated.
32 devices in a mesh: chan: 4 (over y, x), tile: 8 (over z, core).
Axes of the slice: x: 2, y: 2, z: 4, core: 2. Of those that a mesh axis runs over, the one named last changes fastest.
Arguments:
- visibilities: bfloat16 [8192, 1024], P('tile', 'chan'), parts along dimension 1, may hold values from -6 to 6
- send_list: int32 [256, 128], P(('chan', 'tile')), parts along dimension 0, may hold values from -1 to 1023, as said below
- pixels: int32 [2, 32768], P(None, ('chan', 'tile')), parts along dimension 1, may hold values from 0 to 31
- offsets: int32 [2, 32768], P(None, ('chan', 'tile')), parts along dimension 1, may hold values from 0 to 15
- taper: float32 [8, 16], replicated, may hold values from 0.1 to 0.6
Outputs:
- tiles: float32 [8, 32, 32, 1024], P('tile', None, None, 'chan'), parts along dimension 3
There are 4 independent parts, one for each index of `chan`. A program takes and returns all parts, laid end to end along the dimension named above; an argument that names none is the same for every part. Nothing has to cross between parts.
Inputs may be any that keep to these rules, and one draw needn't show every extreme that they name: `send_list`: for every sender and tile the live entries come first and are distinct local row indices; no row is listed twice by one sender; the rest are -1. One tile, drawn from the seed, gets 128 live slots from every sender, and every sender lists its last row.
All inputs are finite; a program needn't handle non-finite values.
Results may differ from a plain program's by a relative error of at most 0.0029.
Values may be sent and summed in bfloat16 or wider, within the bound.
A program may use at most 64 MiB of HBM per device.

v0:
```python
import jax
import jax.numpy as jnp
from jax import lax
from jax.sharding import PartitionSpec as P

TS = 32
TILES_Y = 8


def passed_along(value, axis, by):
    count = lax.axis_size(axis)
    pairs = [(i, i + by) for i in range(count) if 0 <= i + by < count]
    return lax.ppermute(value, axis, pairs)


def spread(kernel, pixel, padded_side):
    cell_index = jnp.arange(padded_side, dtype=jnp.int32)[:, None] - pixel[None, :]
    tap_index = jnp.arange(kernel.shape[0], dtype=jnp.int32)[:, None, None]
    return jnp.sum(jnp.where(cell_index[None] == tap_index, kernel[:, None, :], 0.0), axis=0)


def place_block(block_rows, block_meta, taper, padded_side):
    levels = jnp.arange(taper.shape[1], dtype=jnp.int32)[:, None]
    select_u = (levels == block_meta[2][None, :]).astype(jnp.float32)
    select_v = (levels == block_meta[3][None, :]).astype(jnp.float32)
    kernel_u = jnp.dot(
        taper, select_u, precision=lax.Precision.HIGHEST, preferred_element_type=jnp.float32
    )
    kernel_v = jnp.dot(
        taper, select_v, precision=lax.Precision.HIGHEST, preferred_element_type=jnp.float32
    )
    spread_u = spread(kernel_u, block_meta[0], padded_side)
    spread_v = spread(kernel_v, block_meta[1], padded_side)
    weights = (spread_u[:, None, :] * spread_v[None, :, :]).astype(jnp.bfloat16)
    weights = weights.reshape(padded_side * padded_side, -1)
    return jnp.dot(weights, block_rows, preferred_element_type=jnp.float32)


def grid_blocks(slot_rows, slot_meta, taper, padded_side, block_size, block_count):
    width = slot_rows.shape[1]

    def one_block(index, running):
        start = index * block_size
        block_rows = lax.dynamic_slice_in_dim(slot_rows, start, block_size, 0)
        block_meta = lax.dynamic_slice_in_dim(slot_meta, start, block_size, 1)
        return running + place_block(block_rows, block_meta, taper, padded_side)

    initial = jnp.zeros((padded_side * padded_side, width), jnp.float32)
    return lax.fori_loop(0, block_count, one_block, initial)


def body(visibilities, send_list, pixels, offsets, taper):
    tile_count = lax.axis_size("tile")
    tiles_x = tile_count // TILES_Y
    slot_cap = send_list.shape[1]
    components = visibilities.shape[1]
    padded_side = TS + 8
    slot_total = tile_count * slot_cap
    block_size = min(512, slot_total)
    is_live = send_list >= 0
    picked = jnp.where(is_live, send_list, 0).reshape(-1)
    gathered = jnp.take(visibilities, picked, axis=0).reshape(tile_count, slot_cap, components)
    outgoing = jnp.where(is_live[:, :, None], gathered, jnp.zeros_like(gathered))
    live_flag = is_live.reshape(1, -1)
    slot_meta = jnp.concatenate(
        [
            jnp.take(pixels, picked, axis=1),
            jnp.take(offsets, picked, axis=1),
            live_flag.astype(jnp.int32),
        ],
        0,
    )
    slot_meta = (
        jnp.where(live_flag, slot_meta, 0).reshape(5, tile_count, slot_cap).transpose(1, 0, 2)
    )
    arrived_meta = lax.all_to_all(slot_meta, "tile", split_axis=0, concat_axis=0, tiled=True)
    meta_rows = arrived_meta.transpose(1, 0, 2).reshape(5, slot_total)
    arrived = lax.all_to_all(outgoing, "tile", split_axis=0, concat_axis=0, tiled=True)
    padded_grid = grid_blocks(
        arrived.reshape(slot_total, components),
        meta_rows,
        taper,
        padded_side,
        block_size,
        slot_total // block_size,
    )
    padded_grid = padded_grid.reshape(padded_side, padded_side, components)
    tile_row = lax.axis_index("tile") % TILES_Y
    source_start = {-1: TS + 4, 0: 4, 1: 0}
    target_start = {-1: 0, 0: 0, 1: TS - 4}
    span = {-1: 4, 0: TS, 1: 4}
    result = padded_grid[4 : TS + 4, 4 : TS + 4]
    for step_x in (-1, 0, 1):
        for step_y in (-1, 0, 1):
            if step_x == 0 and step_y == 0 or (step_x != 0 and tiles_x == 1):
                continue
            piece = padded_grid[
                source_start[step_x] : source_start[step_x] + span[step_x],
                source_start[step_y] : source_start[step_y] + span[step_y],
            ]
            incoming = passed_along(piece, "tile", -(step_x * TILES_Y + step_y))
            inside = (tile_row + step_y >= 0) & (tile_row + step_y < TILES_Y)
            incoming = jnp.where(inside, incoming, 0.0)
            result = result.at[
                target_start[step_x] : target_start[step_x] + span[step_x],
                target_start[step_y] : target_start[step_y] + span[step_y],
            ].add(incoming)
    return result[None]


def solution(mesh):
    placed = (
        P("tile", "chan"),
        P(("chan", "tile"), None),
        P(None, ("chan", "tile")),
        P(None, ("chan", "tile")),
        P(),
    )
    return jax.shard_map(
        body, mesh=mesh, in_specs=placed, out_specs=P("tile", None, None, "chan"), check_vma=False
    )
```

profile of v0, /device:TPU:1, one launch (start us, length us, event | category | flops | bytes accessed | tf_op | source)
XLA Modules:
  0.0 58.9 jit_solution(12728926679549928778)
XLA Ops:
  0.0 0.0 copy-start
  0.0 0.8 %compare_and_fusion.1 = (pred[8,128]{1,0:T(8,128)(4,1)S(1)}, s32[8,128]{1,0:T(8,128)S(1)}, pred[8,128]{1,0:T(8,128)(4,1)S(1)}) fusion(s32[8,128]{1,0:T(8,128)} %param.14), kind=kLoop, calls=%fused_computation.34 | loop fusion | flops 8192 | bytes 10240 | tf_op jit(solution)/shard_map/jit(_take)/and | solution.py:62
  0.8 0.9 %copy.15 = s32[2,1024]{0,1:T(8,128)S(1)} copy(s32[2,1024]{1,0:T(2,128)} %param.15) | data formatting | bytes 16384 | tf_op args[2]
  1.7 0.9 %copy.16 = s32[2,1024]{0,1:T(8,128)S(1)} copy(s32[2,1024]{1,0:T(2,128)} %param.16) | data formatting | bytes 16384 | tf_op args[3]
  2.6 2.8 %gather_fusion.1 = s32[1024,2]{1,0:T(8,128)S(1)} fusion(s32[2,1024]{0,1:T(8,128)S(1)} %copy.15, s32[1024]{0:T(1024)S(1)} %fusion.8), kind=kCustom, calls=%fused_computation.clone | custom fusion | bytes 20480 | tf_op jit(solution)/shard_map/jit(_take)/gather | solution.py:67
  5.4 2.8 %gather_fusion.2 = s32[1024,2]{1,0:T(8,128)S(1)} fusion(s32[2,1024]{0,1:T(8,128)S(1)} %copy.16, s32[1024]{0:T(1024)S(1)} %fusion.8), kind=kCustom, calls=%fused_computation.1.clone | custom fusion | bytes 20480 | tf_op jit(solution)/shard_map/jit(_take)/gather | solution.py:68
  8.3 0.2 broadcast_select_fusion.1
  8.5 0.2 copy.18
  8.7 0.2 copy.17
  8.9 0.6 %fusion.7 = s32[8,5,128]{2,1,0:T(8,128)} fusion(s32[1,8,128]{2,0,1:T(1,128)S(1)} %bitcast.76, s32[2,8,128]{2,0,1:T(2,128)S(1)} %copy.18, s32[2,8,128]{2,0,1:T(2,128)S(1)} %copy.17, pred[8,128]{1,0:T(8,128)(4,1)S(1)} %get-tuple-element.155), kind=kLoop, calls=%fused_computation.29 | loop fusion | flops 15360 | bytes 41984 | tf_op jit(solution)/shard_map/transpose | solution.py:74
  9.5 6.4 %all-to-all-start = ((s32[8,5,128]{2,1,0:T(8,128)}), s32[8,5,128]{2,1,0:T(8,128)S(1)}, u32[]{:S(2)}, u32[]{:S(2)}) async-start(s32[8,5,128]{2,1,0:T(8,128)} %fusion.7), calls=%async_computation | async-start | bytes 65536 | tf_op jit(solution)/shard_map/all_to_all | solution.py:76
  15.9 0.0 copy-done
  15.9 3.9 %gather_fusion = bf16[1024,256]{1,0:T(8,128)(2,1)S(1)} fusion(bf16[1024,256]{1,0:T(8,128)(2,1)S(1)} %copy-done, s32[1024]{0:T(1024)S(1)} %broadcast_clamp_fusion), kind=kCustom, calls=%fused_computation.2 | custom fusion | bytes 1052672 | tf_op jit(solution)/shard_map/jit(_take)/gather | solution.py:62
  19.9 0.0 copy-start.1
  19.9 1.1 %select_select_fusion = bf16[8,128,256]{2,1,0:T(8,128)(2,1)} fusion(bf16[8,128,256]{2,1,0:T(8,128)(2,1)S(1)} %bitcast.68, pred[8,128]{1,0:T(8,128)(4,1)S(1)} %get-tuple-element.153, pred[8,128]{1,0:T(8,128)(4,1)S(1)} %get-tuple-element.155), kind=kLoop, calls=%fused_computation.20 | loop fusion | flops 524288 | bytes 1050624 | tf_op jit(solution)/shard_map/jit(_where)/select_n | solution.py:63
  21.0 0.0 all-to-all-done
  21.0 5.1 %all-to-all-start.1 = ((bf16[8,128,256]{2,1,0:T(8,128)(2,1)}), bf16[8,128,256]{2,1,0:T(8,128)(2,1)S(1)}, u32[]{:S(2)}, u32[]{:S(2)}) async-start(bf16[8,128,256]{2,1,0:T(8,128)(2,1)} %select_select_fusion), calls=%async_computation.1 | async-start | bytes 1048576 | tf_op jit(solution)/shard_map/all_to_all | solution.py:78
  26.1 14.5 %all-to-all-done.1 = bf16[8,128,256]{2,1,0:T(8,128)(2,1)S(1)} async-done(((bf16[8,128,256]{2,1,0:T(8,128)(2,1)}), bf16[8,128,256]{2,1,0:T(8,128)(2,1)S(1)}, u32[]{:S(2)}, u32[]{:S(2)}) %all-to-all-start.1) | async-done | bytes 524320 | tf_op jit(solution)/shard_map/all_to_all | solution.py:78
  40.6 0.0 copy-done.1
  40.6 6.9 %while.16 = (s32[]{:T(128)}, f32[1600,256]{1,0:T(8,128)}, s32[5,1024]{1,0:T(8,128)S(1)}, f32[8,16]{1,0:T(8,128)S(1)}, bf16[1024,256]{1,0:T(8,128)(2,1)S(1)}, /*i...) while((s32[]{:T(128)}, f32[1600,256]{1,0:T(8,128)}, ...), condition=%wide.region_3.5_spmd.clone, body=%wide.region_0.4_spmd.clone.sunk | while | flops 424460288 | bytes 7562477 | solution.py:49
  40.6 0.1 constant_dynamic-slice_fusion.2
  40.7 0.1 convolution_bitcast_fusion.4
  40.8 0.1 convolution_bitcast_fusion.5
  41.0 0.1 select_reduce_fusion.3
  41.1 0.4 multiply_convert_fusion.2
  41.5 1.8 %convolution_add_fusion.2 = f32[1600,256]{1,0:T(8,128)} fusion(bf16[1600,512]{1,0:T(8,128)(2,1)S(1)} %bitcast.60, f32[1600,256]{1,0:T(8,128)} %get-tuple-element.222, pred[]{:T(512)S(6)} %compare.15, bf16[1024,256]{1,0:T(8,128)(2,1)S(1)} %get-tuple-element.237, s32[]{:T(128)S(6)} %select_n.134), kind=kOutput, calls=%fused_computation.4.clone.1 | convolution fusion | flops 420249600 | bytes 5177349 | tf_op jit(solution)/shard_map/while/body/eval_jaxpr/dot_general | solution.py:36
  43.3 0.1 constant_dynamic-slice_fusion.2
  43.4 0.1 convolution_bitcast_fusion.4
  43.6 0.1 convolution_bitcast_fusion.5
  43.7 0.1 select_reduce_fusion.3
  43.8 0.4 multiply_convert_fusion.2
  44.2 3.2 %convolution_add_fusion.2 = f32[1600,256]{1,0:T(8,128)} fusion(bf16[1600,512]{1,0:T(8,128)(2,1)S(1)} %bitcast.60, f32[1600,256]{1,0:T(8,128)} %get-tuple-element.222, pred[]{:T(512)S(6)} %compare.15, bf16[1024,256]{1,0:T(8,128)(2,1)S(1)} %get-tuple-element.237, s32[]{:T(128)S(6)} %select_n.134), kind=kOutput, calls=%fused_computation.4.clone.1 | convolution fusion | flops 420249600 | bytes 5177349 | tf_op jit(solution)/shard_map/while/body/eval_jaxpr/dot_general | solution.py:36
  47.5 1.1 %fusion.9 = (f32[32,4,256]{2,1,0:T(4,128)S(1)}, f32[32,4,256]{2,1,0:T(4,128)S(1)}) fusion(f32[40,40,256]{2,1,0:T(8,128)} %bitcast.61), kind=kLoop, calls=%fused_computation.39 | loop fusion | bytes 524288 | tf_op jit(solution)/shard_map/slice | solution.py:97
  48.5 1.9 %collective-permute-start = (f32[32,4,256]{2,1,0:T(4,128)S(1)}, f32[32,4,256]{2,1,0:T(4,128)S(1)}, u32[]{:S(2)}, u32[]{:S(2)}) collective-permute-start(f32[32,4,256]{2,1,0:T(4,128)S(1)} %get-tuple-element.163), channel_id=1, source_target_pairs={{0,1},{1,2},{2,3},{3,4},{4,5},{5,6},{6,7},{8,9},{9,10},{10,11},{11... | collective-permute-start | bytes 393224 | tf_op jit(solution)/shard_map/ppermute | solution.py:13
  50.5 1.5 %slice.107 = f32[32,32,256]{2,1,0:T(8,128)S(1)} slice(f32[40,40,256]{2,1,0:T(8,128)} %bitcast.62), slice={[4:36], [4:36], [0:256]} | slice | bytes 2097152 | tf_op jit(solution)/shard_map/slice | solution.py:92
  52.0 2.4 %collective-permute-start.1 = (f32[32,4,256]{2,1,0:T(4,128)S(1)}, f32[32,4,256]{2,1,0:T(4,128)S(1)}, u32[]{:S(2)}, u32[]{:S(2)}) collective-permute-start(f32[32,4,256]{2,1,0:T(4,128)S(1)} %get-tuple-element.162), channel_id=1, source_target_pairs={{1,0},{2,1},{3,2},{4,3},{5,4},{6,5},{7,6},{9,8},{10,9},{11,10},{12... | collective-permute-start | bytes 393224 | tf_op jit(solution)/shard_map/ppermute | solution.py:13
  54.4 0.0 collective-permute-done
  54.4 1.0 %fusion.6 = f32[32,32,256]{2,1,0:T(8,128)S(1)} fusion(f32[32,32,256]{2,1,0:T(8,128)S(1)} %slice.107, f32[40,40,256]{2,1,0:T(8,128)} %bitcast.63, f32[32,4,256]{2,1,0:T(4,128)S(1)} %collective-permute-done, pred[]{:T(512)S(6)} %and.32), kind=kLoop, calls=%fused_computation.27 | loop fusion | flops 65536 | bytes 393217 | tf_op jit(solution)/shard_map/scatter-add | solution.py:107
  55.4 1.0 %copy.26 = f32[1,32,32,256]{3,2,1,0:T(8,128)} copy(f32[1,32,32,256]{3,2,1,0:T(8,128)S(1)} %bitcast.65) | data formatting | bytes 2097152
  56.4 1.9 %collective-permute-done.1 = f32[32,4,256]{2,1,0:T(4,128)S(1)} collective-permute-done((f32[32,4,256]{2,1,0:T(4,128)S(1)}, f32[32,4,256]{2,1,0:T(4,128)S(1)}, u32[]{:S(2)}, u32[]{:S(2)}) %collective-permute-start.1) | collective-permute-done | bytes 131104 | tf_op jit(solution)/shard_map/ppermute | solution.py:13
  58.2 0.7 %fusion.5 = f32[1,32,32,256]{3,2,1,0:T(8,128)} fusion(f32[1,32,32,256]{3,2,1,0:T(8,128)} %copy.26, f32[32,32,256]{2,1,0:T(8,128)S(1)} %fusion.6, f32[32,4,256]{2,1,0:T(4,128)S(1)} %collective-permute-done.1, pred[]{:T(512)S(6)} %and.33), kind=kLoop, calls=%fused_computation.25 | loop fusion | flops 65536 | bytes 393217 | tf_op jit(solution)/shard_map/scatter-add | solution.py:107
  (10 shorter events, 0.1 us)
Async XLA Ops:
  0.0 15.9 %copy-start = (bf16[1024,256]{1,0:T(8,128)(2,1)S(1)}, bf16[1024,256]{1,0:T(8,128)(2,1)}, u32[]{:S(2)}) copy-start(bf16[1024,256]{1,0:T(8,128)(2,1)} %param.13) | copy-start | bytes 1572868
  9.5 11.5 %all-to-all-start = ((s32[8,5,128]{2,1,0:T(8,128)}), s32[8,5,128]{2,1,0:T(8,128)S(1)}, u32[]{:S(2)}, u32[]{:S(2)}) async-start(s32[8,5,128]{2,1,0:T(8,128)} %fusion.7), calls=%async_computation | async-start | bytes 65536 | tf_op jit(solution)/shard_map/all_to_all | solution.py:76
  19.9 20.7 %copy-start.1 = (f32[8,16]{1,0:T(8,128)S(1)}, f32[8,16]{1,0:T(8,128)}, u32[]{:S(2)}) copy-start(f32[8,16]{1,0:T(8,128)} %param.17) | copy-start | bytes 1540
  21.0 19.6 %all-to-all-start.1 = ((bf16[8,128,256]{2,1,0:T(8,128)(2,1)}), bf16[8,128,256]{2,1,0:T(8,128)(2,1)S(1)}, u32[]{:S(2)}, u32[]{:S(2)}) async-start(bf16[8,128,256]{2,1,0:T(8,128)(2,1)} %select_select_fusion), calls=%async_computation.1 | async-start | bytes 1048576 | tf_op jit(solution)/shard_map/all_to_all | solution.py:78
  48.5 5.8 %collective-permute-start = (f32[32,4,256]{2,1,0:T(4,128)S(1)}, f32[32,4,256]{2,1,0:T(4,128)S(1)}, u32[]{:S(2)}, u32[]{:S(2)}) collective-permute-start(f32[32,4,256]{2,1,0:T(4,128)S(1)} %get-tuple-element.163), channel_id=1, source_target_pairs={{0,1},{1,2},{2,3},{3,4},{4,5},{5,6},{6,7},{8,9},{9,10},{10,11},{11... | collective-permute-start | bytes 393224 | tf_op jit(solution)/shard_map/ppermute | solution.py:13
  52.0 6.3 %collective-permute-start.1 = (f32[32,4,256]{2,1,0:T(4,128)S(1)}, f32[32,4,256]{2,1,0:T(4,128)S(1)}, u32[]{:S(2)}, u32[]{:S(2)}) collective-permute-start(f32[32,4,256]{2,1,0:T(4,128)S(1)} %get-tuple-element.162), channel_id=1, source_target_pairs={{1,0},{2,1},{3,2},{4,3},{5,4},{6,5},{7,6},{9,8},{10,9},{11,10},{12... | collective-permute-start | bytes 393224 | tf_op jit(solution)/shard_map/ppermute | solution.py:13
where the time goes:
time: 59.4 us; the launch traced here: 58.9 us
  waiting for transfers between devices  16.4 us (28%)
  starting transfers between devices  15.8 us (27%)
  local copies, waits for them, and re-layouts  15.4 us (26%)
  other arithmetic  5.58 us (9%)
  matrix products  5.54 us (9%)
    all_to_all x1, waiting for transfers between devices, body(): lax.all_to_all(outgoing, 'tile', split_axis=0, concat_axis=0, tiled=True)  14.5 us
    all_to_all x1, starting transfers between devices, body(): lax.all_to_all(slot_meta, 'tile', split_axis=0, concat_axis=0, tiled=True)  6.38 us
    all_to_all x1, starting transfers between devices, body(): lax.all_to_all(outgoing, 'tile', split_axis=0, concat_axis=0, tiled=True)  5.1 us
    dot_general x2, matrix products, place_block(): return jnp.dot(weights, block_rows, preferred_element_type=jnp.float32)  5.01 us
    ppermute x2, starting transfers between devices, passed_along(): return lax.ppermute(value, axis, pairs)  4.33 us
    gather x1, local copies, waits for them, and re-layouts, body(): jnp.take(visibilities, picked, axis=0)  3.94 us
    unnamed x7, local copies, waits for them, and re-layouts  2.81 us
    gather x1, local copies, waits for them, and re-layouts, body(): jnp.take(offsets, picked, axis=1)  2.81 us
  transfers between devices with their start and end apart: 4, of which 2 were waited for; matrix products, arithmetic and copies ran while one was open for 14% of the time, Pallas kernels for 0%

commit v1 on v0

--- a/solution.py
+++ b/solution.py
@@ -1,10 +1,237 @@
 import jax
 import jax.numpy as jnp
 from jax import lax
+from jax.experimental import pallas as pl
+from jax.experimental.pallas import tpu as pltpu
 from jax.sharding import PartitionSpec as P
 
 TS = 32
 TILES_Y = 8
+RIM = 4
+LANES = 128
+MESH = pl.DeviceIdType.MESH
+
+
+def flip(index, distance):
+    total = 0
+    for bit in (1, 2, 4):
+        own = (index // bit) % 2
+        total = total + bit * (1 - own if distance & bit else own)
+    return total
+
+
+def line_kernel(
+    vis, lists, pix, off, taper, out,
+    rows_out, rows_in, meta_out, meta_in, w_main, w_rim, rim_sum, rim_out, rim_in,
+    row_send, row_recv, meta_send, meta_recv, rim_send, rim_recv,
+):
+    count, slots = lists.shape
+    rows, width = vis.shape
+    taps, levels = taper.shape
+    me = lax.axis_index("tile")
+    far_first = [d for d in range(count - 1, 1, -1)] + [1]
+    peers = {d: flip(me, d) for d in range(1, count)}
+
+    barrier = pltpu.get_barrier_semaphore()
+    for d in far_first:
+        pl.semaphore_signal(barrier, inc=1, device_id={"tile": peers[d]}, device_id_type=MESH)
+
+    listed = lists[...]
+    live = listed >= 0
+    spot = jnp.where(live, listed, 0)
+    packed = pix[0:1, :] + 32 * pix[1:2, :] + 1024 * off[0:1, :] + 16384 * off[1:2, :]
+    inner = spot & (LANES - 1)
+    outer = spot >> 7
+    found = jnp.zeros((count, slots), jnp.int32)
+    for b in range(rows // LANES):
+        source = jnp.broadcast_to(packed[:, b * LANES : (b + 1) * LANES], (count, LANES))
+        here = jnp.take_along_axis(source, inner, axis=1, mode="promise_in_bounds")
+        found = jnp.where(outer == b, here, found)
+    fields = (
+        jnp.where(live, found & 31, -64),
+        jnp.where(live, (found >> 5) & 31, -64),
+        (found >> 10) & 15,
+        (found >> 14) & 15,
+    )
+    for t in range(count):
+        for f, field in enumerate(fields):
+            meta_out[t, f : f + 1, :] = field[t : t + 1, :]
+
+    pl.semaphore_wait(barrier, count - 1)
+
+    def meta_copy(d):
+        return pltpu.make_async_remote_copy(
+            src_ref=meta_out.at[peers[d]], dst_ref=meta_in.at[me],
+            send_sem=meta_send.at[d], recv_sem=meta_recv.at[d],
+            device_id={"tile": peers[d]}, device_id_type=MESH,
+        )
+
+    def row_copy(d):
+        return pltpu.make_async_remote_copy(
+            src_ref=rows_out.at[d], dst_ref=rows_in.at[me],
+            send_sem=row_send.at[d], recv_sem=row_recv.at[d],
+            device_id={"tile": peers[d]}, device_id_type=MESH,
+        )
+
+    for d in far_first:
+        meta_copy(d).start()
+    meta_in[me] = meta_out[me]
+
+    lane = lax.broadcasted_iota(jnp.int32, (slots, LANES), 1)
+
+    def pick(t):
+        row = lists[pl.ds(t, 1), :]
+        spread_list = jnp.broadcast_to(row, (LANES, slots)).T
+        hot = [
+            jnp.where(spread_list == lane + b * LANES, 1.0, 0.0).astype(jnp.bfloat16)
+            for b in range(rows // LANES)
+        ]
+        return jnp.concatenate(hot, axis=1)
+
+    for d in range(count - 2, -1, -2):
+        near = me if d == 0 else peers[d]
+        hot = jnp.concatenate([pick(near), pick(peers[d + 1])], axis=0)
+        got = jnp.dot(hot, vis[...], preferred_element_type=jnp.float32).astype(jnp.bfloat16)
+        if d == 0:
+            rows_in[me] = got[:slots]
+        else:
+            rows_out[d] = got[:slots]
+            row_copy(d).start()
+        rows_out[d + 1] = got[slots:]
+        row_copy(d + 1).start()
+
+    for d in far_first:
+        meta_copy(d).wait_recv()
+
+    cell = lax.broadcasted_iota(jnp.int32, (TS, slots), 0) + RIM
+    edge = lax.broadcasted_iota(jnp.int32, (2 * RIM, slots), 0)
+    edge = jnp.where(edge >= RIM, edge + TS, edge)
+
+    def spread(kernel, pixel, cells):
+        tap = cells - pixel
+        total = jnp.zeros(cells.shape, jnp.float32)
+        for a in range(taps):
+            total = jnp.where(tap == a, kernel[a : a + 1, :], total)
+        return total
+
+    def build(s, carry):
+        meta = meta_in[s]
+        kernel_u = jnp.zeros((taps, slots), jnp.float32)
+        kernel_v = jnp.zeros((taps, slots), jnp.float32)
+        for o in range(levels):
+            column = jnp.broadcast_to(taper[:, o : o + 1], (taps, slots))
+            kernel_u = jnp.where(meta[2:3, :] == o, column, kernel_u)
+            kernel_v = jnp.where(meta[3:4, :] == o, column, kernel_v)
+        spread_u = spread(kernel_u, meta[0:1, :], cell)
+        spread_v = spread(kernel_v, meta[1:2, :], cell)
+        edge_v = spread(kernel_v, meta[1:2, :], edge)
+        at = pl.ds(pl.multiple_of(s * slots, LANES), slots)
+        for i in range(TS):
+            w_main[i * TS : (i + 1) * TS, at] = (spread_u[i : i + 1, :] * spread_v).astype(
+                jnp.bfloat16
+            )
+        for j in range(2 * RIM):
+            w_rim[j * TS : (j + 1) * TS, at] = (spread_u * edge_v[j : j + 1, :]).astype(
+                jnp.bfloat16
+            )
+        return carry
+
+    lax.fori_loop(0, count, build, 0)
+
+    for d in range(0, count, 2):
+        if d:
+            row_copy(d).wait_recv()
+        row_copy(d + 1).wait_recv()
+        pair = (me if d == 0 else peers[d]) // 2
+        block = rows_in[pl.ds(2 * pair, 2)].reshape(2 * slots, width)
+        at = pl.ds(pl.multiple_of(pair * 2 * slots, 2 * LANES), 2 * slots)
+        term = jnp.dot(w_rim[:, at], block, preferred_element_type=jnp.float32)
+        if d == 0:
+            rim_sum[...] = term
+        elif d < count - 2:
+            rim_sum[...] += term
+        else:
+            whole = (rim_sum[...] + term).astype(jnp.bfloat16)
+            rim_out[0] = whole[: RIM * TS]
+            rim_out[1] = whole[RIM * TS :]
+
+    has_low = me > 0
+    has_high = me < count - 1
+
+    def rim_copy(side):
+        return pltpu.make_async_remote_copy(
+            src_ref=rim_out.at[side], dst_ref=rim_in.at[1 - side],
+            send_sem=rim_send.at[side], recv_sem=rim_recv.at[1 - side],
+            device_id={"tile": me - 1 + 2 * side}, device_id_type=MESH,
+        )
+
+    def rim_arrival(side):
+        return pltpu.make_async_remote_copy(
+            src_ref=rim_out.at[side], dst_ref=rim_in.at[side],
+            send_sem=rim_send.at[side], recv_sem=rim_recv.at[side],
+            device_id={"tile": me - 1 + 2 * side}, device_id_type=MESH,
+        )
+
+    for side, present in ((0, has_low), (1, has_high)):
+        @pl.when(present)
+        def _(side=side):
+            rim_copy(side).start()
+
+    everything = rows_in[...].reshape(count * slots, width)
+    part = TS * TS // 4
+    for m in range(4):
+        total = jnp.dot(
+            w_main[m * part : (m + 1) * part, :], everything, preferred_element_type=jnp.float32
+        )
+        out[m * part // TS : (m + 1) * part // TS] = total.reshape(part // TS, TS, width)
+
+    place = lax.broadcasted_iota(jnp.int32, (8 * TS, RIM * TS), 0)
+    origin = lax.broadcasted_iota(jnp.int32, (8 * TS, RIM * TS), 1)
+    for side, present in ((0, has_low), (1, has_high)):
+        @pl.when(present)
+        def _(side=side):
+            rim_arrival(side).wait_recv()
+            wanted = (origin % TS) * 8 + origin // TS + RIM * side
+            put = jnp.where(place == wanted, 1.0, 0.0).astype(jnp.bfloat16)
+            extra = jnp.dot(put, rim_in[side], preferred_element_type=jnp.float32)
+            first = (TS - 8) * side
+            out[:, first : first + 8, :] += extra.reshape(TS, 8, width)
+            rim_copy(side).wait_send()
+
+    for d in far_first:
+        meta_copy(d).wait_send()
+        row_copy(d).wait_send()
+
+
+def line_body(visibilities, send_list, pixels, offsets, taper):
+    count, slots = send_list.shape
+    width = visibilities.shape[1]
+    cells = TS * TS
+    rim_cells = 2 * RIM * TS
+    dma = pltpu.SemaphoreType.DMA
+    vmem = pl.BlockSpec(memory_space=pltpu.VMEM)
+    result = pl.pallas_call(
+        line_kernel,
+        out_shape=jax.ShapeDtypeStruct((TS, TS, width), jnp.float32),
+        in_specs=[vmem] * 5,
+        out_specs=vmem,
+        scratch_shapes=[
+            pltpu.VMEM((count, slots, width), jnp.bfloat16),
+            pltpu.VMEM((count, slots, width), jnp.bfloat16),
+            pltpu.VMEM((count, 8, slots), jnp.int32),
+            pltpu.VMEM((count, 8, slots), jnp.int32),
+            pltpu.VMEM((cells, count * slots), jnp.bfloat16),
+            pltpu.VMEM((rim_cells, count * slots), jnp.bfloat16),
+            pltpu.VMEM((rim_cells, width), jnp.float32),
+            pltpu.VMEM((2, rim_cells // 2, width), jnp.bfloat16),
+            pltpu.VMEM((2, rim_cells // 2, width), jnp.bfloat16),
+            dma((count,)), dma((count,)), dma((count,)), dma((count,)), dma((2,)), dma((2,)),
+        ],
+        compiler_params=pltpu.CompilerParams(
+            collective_id=0, has_side_effects=True, vmem_limit_bytes=48 * 1024 * 1024
+        ),
+    )(visibilities, send_list, pixels, offsets, taper)
+    return result[None]
 
 
 def passed_along(value, axis, by):
@@ -116,6 +343,12 @@
         P(None, ("chan", "tile")),
         P(),
     )
+    one_line = mesh.shape["tile"] == TILES_Y
+
+    def chosen(visibilities, send_list, *rest):
+        fits = one_line and send_list.shape[1] == LANES and visibilities.shape[0] % LANES == 0
+        return (line_body if fits else body)(visibilities, send_list, *rest)
+
     return jax.shard_map(
-        body, mesh=mesh, in_specs=placed, out_specs=P("tile", None, None, "chan"), check_vma=False
-    )
+        chosen, mesh=mesh, in_specs=placed, out_specs=P("tile", None, None, "chan"), check_vma=False
+    )

time: 59.4 us -> 25.4 us (0.43)
  the two profiles are of different devices: /device:TPU:1 before, /device:TPU:21 now
where the time goes in v1:
time: 25.4 us; the launch traced here: 25.1 us
  Pallas kernels  20.3 us (80%)
  local copies, waits for them, and re-layouts  4.78 us (19%)
    pallas_call x1, Pallas kernels, line_body(): pl.pallas_call(line_kernel, out_shape=jax.ShapeDtypeStruct((TS, TS, width...  20.3 us
    unnamed x11, local copies, waits for them, and re-layouts  4.78 us

profile of v1, /device:TPU:21, one launch (start us, length us, event | category | flops | bytes accessed | tf_op | source)
XLA Modules:
  0.0 25.1 jit_solution(14277406480351559708)
XLA Ops:
  0.0 0.0 copy-start
  0.0 1.0 %copy-done = bf16[1024,256]{1,0:T(8,128)(2,1)S(1)} copy-done((bf16[1024,256]{1,0:T(8,128)(2,1)S(1)}, bf16[1024,256]{1,0:T(8,128)(2,1)}, u32[]{:S(2)}) %copy-start) | copy-done | bytes 524312
  1.0 0.0 copy-start.1
  1.0 0.7 %copy-done.1 = s32[2,1024]{1,0:T(2,128)S(1)} copy-done((s32[2,1024]{1,0:T(2,128)S(1)}, s32[2,1024]{1,0:T(2,128)}, u32[]{:S(2)}) %copy-start.1) | copy-done | bytes 8216
  1.7 0.0 copy-start.2
  1.7 0.7 %copy-done.2 = s32[2,1024]{1,0:T(2,128)S(1)} copy-done((s32[2,1024]{1,0:T(2,128)S(1)}, s32[2,1024]{1,0:T(2,128)}, u32[]{:S(2)}) %copy-start.2) | copy-done | bytes 8216
  2.4 0.0 copy-start.3
  2.4 0.7 %copy-done.3 = s32[8,128]{1,0:T(8,128)S(1)} copy-done((s32[8,128]{1,0:T(8,128)S(1)}, s32[8,128]{1,0:T(8,128)}, u32[]{:S(2)}) %copy-start.3) | copy-done | bytes 4120
  3.1 0.0 copy-start.4
  3.1 0.7 %copy-done.4 = f32[8,16]{1,0:T(8,128)S(1)} copy-done((f32[8,16]{1,0:T(8,128)S(1)}, f32[8,16]{1,0:T(8,128)}, u32[]{:S(2)}) %copy-start.4) | copy-done | bytes 536
  3.8 20.3 %shard_map.55 = f32[32,32,256]{2,1,0:T(8,128)S(1)} custom-call(bf16[1024,256]{1,0:T(8,128)(2,1)S(1)} %copy-done, s32[8,128]{1,0:T(8,128)S(1)} %copy-done.3, s32[2,1024]{1,0:T(2,128)S(1)} %copy-done.1, s32[2,1024]{1,0:T(2,128)S(1)} %copy-done.2, f32[8,16]{1,0:T(8,128)S(1)} %copy-done.4), custom_call_target="tpu_custom_call" | custom-call | tf_op jit(solution)/shard_map/pallas_call | solution.py:213
  24.1 1.0 %copy.7 = f32[1,32,32,256]{3,2,1,0:T(8,128)} copy(f32[1,32,32,256]{3,2,1,0:T(8,128)S(1)} %bitcast.1) | data formatting | bytes 2097152
Async XLA Ops:
  0.0 1.0 %copy-start = (bf16[1024,256]{1,0:T(8,128)(2,1)S(1)}, bf16[1024,256]{1,0:T(8,128)(2,1)}, u32[]{:S(2)}) copy-start(bf16[1024,256]{1,0:T(8,128)(2,1)} %vis.1) | copy-start | bytes 1572868
  1.0 0.7 %copy-start.1 = (s32[2,1024]{1,0:T(2,128)S(1)}, s32[2,1024]{1,0:T(2,128)}, u32[]{:S(2)}) copy-start(s32[2,1024]{1,0:T(2,128)} %pix.1) | copy-start | bytes 24580
  1.7 0.7 %copy-start.2 = (s32[2,1024]{1,0:T(2,128)S(1)}, s32[2,1024]{1,0:T(2,128)}, u32[]{:S(2)}) copy-start(s32[2,1024]{1,0:T(2,128)} %off.1) | copy-start | bytes 24580
  2.4 0.7 %copy-start.3 = (s32[8,128]{1,0:T(8,128)S(1)}, s32[8,128]{1,0:T(8,128)}, u32[]{:S(2)}) copy-start(s32[8,128]{1,0:T(8,128)} %lists.1) | copy-start | bytes 12292
  3.1 0.7 %copy-start.4 = (f32[8,16]{1,0:T(8,128)S(1)}, f32[8,16]{1,0:T(8,128)}, u32[]{:S(2)}) copy-start(f32[8,16]{1,0:T(8,128)} %taper.1) | copy-start | bytes 1540

commit v2 on v1

--- a/solution.py
+++ b/solution.py
@@ -21,8 +21,8 @@
 
 
 def line_kernel(
-    vis, lists, pix, off, taper, out,
-    rows_out, rows_in, meta_out, meta_in, w_main, w_rim, rim_sum, rim_out, rim_in,
+    vis_far, lists_far, pix_far, off_far, taper_far, out,
+    vis, lists, pix, off, taper, load_sem, rows_out, rows_in, meta_out, meta_in, w_main, w_rim, rim_sum, rim_out, rim_in,
     row_send, row_recv, meta_send, meta_recv, rim_send, rim_recv,
 ):
     count, slots = lists.shape
@@ -35,7 +35,17 @@
     barrier = pltpu.get_barrier_semaphore()
     for d in far_first:
         pl.semaphore_signal(barrier, inc=1, device_id={"tile": peers[d]}, device_id_type=MESH)
-
+    loads = [
+        pltpu.make_async_copy(far, near, load_sem.at[i])
+        for i, (far, near) in enumerate(
+            ((lists_far, lists), (pix_far, pix), (off_far, off), (taper_far, taper), (vis_far, vis))
+        )
+    ]
+    for load in loads:
+        load.start()
+
+    for load in loads[:4]:
+        load.wait()
     listed = lists[...]
     live = listed >= 0
     spot = jnp.where(live, listed, 0)
@@ -57,11 +67,9 @@
         for f, field in enumerate(fields):
             meta_out[t, f : f + 1, :] = field[t : t + 1, :]
 
-    pl.semaphore_wait(barrier, count - 1)
-
     def meta_copy(d):
         return pltpu.make_async_remote_copy(
-            src_ref=meta_out.at[peers[d]], dst_ref=meta_in.at[me],
+            src_ref=meta_out.at[peers[d], 0:4], dst_ref=meta_in.at[me, 0:4],
             send_sem=meta_send.at[d], recv_sem=meta_recv.at[d],
             device_id={"tile": peers[d]}, device_id_type=MESH,
         )
@@ -72,10 +80,6 @@
             send_sem=row_send.at[d], recv_sem=row_recv.at[d],
             device_id={"tile": peers[d]}, device_id_type=MESH,
         )
-
-    for d in far_first:
-        meta_copy(d).start()
-    meta_in[me] = meta_out[me]
 
     lane = lax.broadcasted_iota(jnp.int32, (slots, LANES), 1)
 
@@ -88,16 +92,23 @@
         ]
         return jnp.concatenate(hot, axis=1)
 
+    loads[4].wait()
     for d in range(count - 2, -1, -2):
         near = me if d == 0 else peers[d]
         hot = jnp.concatenate([pick(near), pick(peers[d + 1])], axis=0)
         got = jnp.dot(hot, vis[...], preferred_element_type=jnp.float32).astype(jnp.bfloat16)
+        rows_out[d + 1] = got[slots:]
         if d == 0:
             rows_in[me] = got[:slots]
         else:
             rows_out[d] = got[:slots]
+        if d == count - 2:
+            pl.semaphore_wait(barrier, count - 1)
+            for e in far_first:
+                meta_copy(e).start()
+            meta_in[me] = meta_out[me]
+        if d:
             row_copy(d).start()
-        rows_out[d + 1] = got[slots:]
         row_copy(d + 1).start()
 
     for d in far_first:
@@ -212,10 +223,16 @@
     vmem = pl.BlockSpec(memory_space=pltpu.VMEM)
     result = pl.pallas_call(
         line_kernel,
-        out_shape=jax.ShapeDtypeStruct((TS, TS, width), jnp.float32),
-        in_specs=[vmem] * 5,
+        out_shape=pltpu.VMEM((TS, TS, width), jnp.float32),
+        in_specs=[pl.BlockSpec(memory_space=pltpu.HBM)] * 5,
         out_specs=vmem,
         scratch_shapes=[
+            pltpu.VMEM(visibilities.shape, visibilities.dtype),
+            pltpu.VMEM(send_list.shape, send_list.dtype),
+            pltpu.VMEM(pixels.shape, pixels.dtype),
+            pltpu.VMEM(offsets.shape, offsets.dtype),
+            pltpu.VMEM(taper.shape, taper.dtype),
+            dma((5,)),
             pltpu.VMEM((count, slots, width), jnp.bfloat16),
             pltpu.VMEM((count, slots, width), jnp.bfloat16),
             pltpu.VMEM((count, 8, slots), jnp.int32),
@@ -230,7 +247,10 @@
         compiler_params=pltpu.CompilerParams(
             collective_id=0, has_side_effects=True, vmem_limit_bytes=48 * 1024 * 1024
         ),
-    )(visibilities, send_list, pixels, offsets, taper)
+    )(*(
+        pltpu.with_memory_space_constraint(x, pltpu.HBM)
+        for x in (visibilities, send_list, pixels, offsets, taper)
+    ))
     return result[None]
 
 

time: 25.4 us -> 20.8 us (0.82)
  the two profiles are of different devices: /device:TPU:21 before, /device:TPU:1 now
where the time goes in v2:
time: 20.8 us; the launch traced here: 20.6 us
  Pallas kernels  19.6 us (94%)
  local copies, waits for them, and re-layouts  0.97 us (5%)
    pallas_call x1, Pallas kernels, line_body(): pl.pallas_call(line_kernel, out_shape=pltpu.VMEM((TS, TS, width), jnp.flo...  19.6 us
    unnamed x1, local copies, waits for them, and re-layouts  0.97 us

profile of v2, /device:TPU:1, one launch (start us, length us, event | category | flops | bytes accessed | tf_op | source)
XLA Modules:
  0.0 20.6 jit_solution(6724241265281196413)
XLA Ops:
  0.0 19.6 %shard_map.55 = f32[32,32,256]{2,1,0:T(8,128)S(1)} custom-call(bf16[1024,256]{1,0:T(8,128)(2,1)} %vis_far.1, s32[8,128]{1,0:T(8,128)} %lists_far.1, s32[2,1024]{1,0:T(2,128)} %pix_far.1, s32[2,1024]{1,0:T(2,128)} %off_far.1, f32[8,16]{1,0:T(8,128)} %taper_far.1), custom_call_target="tpu_custom_call" | custom-call | tf_op jit(solution)/shard_map/pallas_call | solution.py:224
  19.6 1.0 %copy.7 = f32[1,32,32,256]{3,2,1,0:T(8,128)} copy(f32[1,32,32,256]{3,2,1,0:T(8,128)S(1)} %bitcast.1) | data formatting | bytes 2097152

commit v3 on v2

--- a/solution.py
+++ b/solution.py
@@ -93,7 +93,7 @@
         return jnp.concatenate(hot, axis=1)
 
     loads[4].wait()
-    for d in range(count - 2, -1, -2):
+    for d in (6, 4):
         near = me if d == 0 else peers[d]
         hot = jnp.concatenate([pick(near), pick(peers[d + 1])], axis=0)
         got = jnp.dot(hot, vis[...], preferred_element_type=jnp.float32).astype(jnp.bfloat16)
@@ -102,14 +102,23 @@
             rows_in[me] = got[:slots]
         else:
             rows_out[d] = got[:slots]
-        if d == count - 2:
-            pl.semaphore_wait(barrier, count - 1)
-            for e in far_first:
-                meta_copy(e).start()
-            meta_in[me] = meta_out[me]
-        if d:
-            row_copy(d).start()
-        row_copy(d + 1).start()
+    pl.semaphore_wait(barrier, count - 1)
+    for e in far_first:
+        meta_copy(e).start()
+    meta_in[me] = meta_out[me]
+    for d in (6, 4, 7, 5):
+        row_copy(d).start()
+    for d in (2, 0):
+        near = me if d == 0 else peers[d]
+        hot = jnp.concatenate([pick(near), pick(peers[d + 1])], axis=0)
+        got = jnp.dot(hot, vis[...], preferred_element_type=jnp.float32).astype(jnp.bfloat16)
+        rows_out[d + 1] = got[slots:]
+        if d == 0:
+            rows_in[me] = got[:slots]
+        else:
+            rows_out[d] = got[:slots]
+    for d in (2, 3, 1):
+        row_copy(d).start()
 
     for d in far_first:
         meta_copy(d).wait_recv()

time: 20.8 us -> 20.7 us (level)
  no operation moved by 1% of the time
where the time goes in v3:
time: 20.7 us; the launch traced here: 20.6 us
  Pallas kernels  19.6 us (95%)
  local copies, waits for them, and re-layouts  0.97 us (5%)
    pallas_call x1, Pallas kernels, line_body(): pl.pallas_call(line_kernel, out_shape=pltpu.VMEM((TS, TS, width), jnp.flo...  19.6 us
    unnamed x1, local copies, waits for them, and re-layouts  0.97 us

profile of v3, /device:TPU:1, one launch (start us, length us, event | category | flops | bytes accessed | tf_op | source)
XLA Modules:
  0.0 20.6 jit_solution(1267822098916428846)
XLA Ops:
  0.0 19.6 %shard_map.55 = f32[32,32,256]{2,1,0:T(8,128)S(1)} custom-call(bf16[1024,256]{1,0:T(8,128)(2,1)} %vis_far.1, s32[8,128]{1,0:T(8,128)} %lists_far.1, s32[2,1024]{1,0:T(2,128)} %pix_far.1, s32[2,1024]{1,0:T(2,128)} %off_far.1, f32[8,16]{1,0:T(8,128)} %taper_far.1), custom_call_target="tpu_custom_call" | custom-call | tf_op jit(solution)/shard_map/pallas_call | solution.py:233
  19.6 1.0 %copy.7 = f32[1,32,32,256]{3,2,1,0:T(8,128)} copy(f32[1,32,32,256]{3,2,1,0:T(8,128)S(1)} %bitcast.1) | data formatting | bytes 2097152
